TPU v7x, 256 devices: a whole 4x4x8 slice. The times are simulated.
256 devices in a mesh: views: 16 (over x, y), rows: 16 (over z, core).
Axes of the slice: x: 4, y: 4, z: 8, core: 2. Of those that a mesh axis runs over, the one named last changes fastest.
Arguments:
- grad_par: bfloat16 [256, 512, 2048], P('views', None, 'rows'), may hold values from -4 to 12
- contrib_owner: int32 [256, 1], P('views'), may hold values from 0 to 15; in each aligned block of 16 rows (0 to 15, 16 to 31, ...) at most 2 rows name the same one
- contrib_fan: int32 [256], P('views'), may hold values from 0 to 15
- contrib_start: int32 [256], P('views'), may hold values from 0 to 14
- contrib_wt: bfloat16 [256, 2], P('views'), may hold values from 0.19921875 to 1
Outputs:
- fan_grad: bfloat16 [256, 512, 2048], P('views', 'rows')
Inputs may be any that keep to these rules, and one draw needn't show every extreme that they name: `contrib_owner`: among the 16 entries of one view group, no owner group is named more than 2 times.
All inputs are finite; a program needn't handle non-finite values.
Results may differ from a plain program's by a relative error of at most 0.001.
The roundings to bfloat16 on the way count: a program that leaves them out, or rounds other values in their place, can miss the bound.
Values may be sent and summed in bfloat16 or wider, within the bound.
A program may use at most 64 MiB of HBM per device.

v0:
```python
import math

import jax
import jax.numpy as jnp
from jax import lax
from jax.sharding import PartitionSpec as P


def ramp_matrix(channels):
    positions = lax.iota(jnp.int32, channels)
    distance = jnp.abs(positions[:, None] - positions[None, :])
    far_float = jnp.maximum(distance.astype(jnp.float32), jnp.float32(1.0))
    odd_values = jnp.float32(-4.0) / (jnp.float32(math.pi**2) * far_float * far_float)
    values = jnp.where(
        distance == 0, jnp.float32(1.0), jnp.where(distance % 2 == 1, odd_values, jnp.float32(0.0))
    )
    return values.astype(jnp.bfloat16)


def on_device(grad_par, contrib_owner, contrib_fan, contrib_start, contrib_wt):
    groups = lax.axis_size("views")
    local_views = grad_par.shape[0]
    channels = grad_par.shape[2] * lax.axis_size("rows")
    filter_table = ramp_matrix(channels)
    view_block = lax.all_to_all(grad_par, "rows", split_axis=1, concat_axis=2, tiled=True)
    flattened = view_block.reshape(-1, channels)
    result_rows = jnp.dot(flattened, filter_table, preferred_element_type=jnp.float32)
    filtered = result_rows.astype(jnp.bfloat16).reshape(view_block.shape)
    row_count = filtered.shape[1]
    contribs = contrib_owner.shape[0]
    band_len = contrib_wt.shape[1]
    capacity = 2 * contribs // groups
    slots_all = groups * capacity
    owner_ids = contrib_owner[:, 0]
    owner_hot = (owner_ids[:, None] == lax.iota(jnp.int32, groups)[None, :]).astype(jnp.int32)
    earlier = jnp.cumsum(owner_hot, axis=0) - owner_hot
    position = owner_ids * capacity + jnp.sum(earlier * owner_hot, axis=1)
    dispatch = (lax.iota(jnp.int32, slots_all)[:, None] == position[None, :]).astype(jnp.float32)
    fan_code = (contrib_fan + 1).astype(jnp.float32)
    columns = jnp.concatenate([fan_code[:, None], contrib_wt.astype(jnp.float32)], axis=1)
    slot_info = jnp.dot(dispatch, columns, precision=lax.Precision.HIGHEST)
    received_info = lax.all_to_all(
        slot_info.reshape(groups, capacity, 1 + band_len),
        "views",
        split_axis=0,
        concat_axis=0,
        tiled=True,
    )
    target = received_info[:, :, 0].reshape(-1).astype(jnp.int32) - 1
    collect = (lax.iota(jnp.int32, local_views)[:, None] == target[None, :]).astype(jnp.bfloat16)
    band_views = (contrib_start[:, None] + lax.iota(jnp.int32, band_len)[None, :]).astype(
        jnp.float32
    )
    slot_views = jnp.dot(dispatch, band_views, precision=lax.Precision.HIGHEST).astype(jnp.int32)
    chosen = jnp.take(filtered, slot_views.reshape(-1), axis=0)
    chosen = chosen.reshape(groups, capacity * band_len, row_count, channels)
    weights = received_info[:, :, 1:].astype(jnp.bfloat16).reshape(slots_all, band_len)
    received = lax.all_to_all(chosen, "views", split_axis=0, concat_axis=0, tiled=True)
    rows_here = received.shape[2]
    paired = received.reshape(slots_all, band_len, rows_here * channels)
    blended = jnp.einsum("sb,sbk->sk", weights, paired, preferred_element_type=jnp.float32).astype(
        jnp.bfloat16
    )
    summed = jnp.dot(collect, blended, preferred_element_type=jnp.float32)
    return summed.astype(jnp.bfloat16).reshape(local_views, rows_here, channels)


def solution(mesh):
    return jax.shard_map(
        on_device,
        mesh=mesh,
        in_specs=(
            P("views", None, "rows"),
            P("views", None),
            P("views"),
            P("views"),
            P("views", None),
        ),
        out_specs=P("views", "rows", None),
        check_vma=False,
    )
```

profile of v0, /device:TPU:1, one launch (start us, length us, event | category | flops | bytes accessed | tf_op | source)
XLA Modules:
  0.0 292.6 jit_solution(7416435775941764799)
XLA Ops:
  0.0 0.0 copy-start
  0.0 0.0 copy-start.1
  0.0 0.0 copy-start.2
  0.0 0.0 copy-start.3
  0.0 4.3 %copy.14 = bf16[16,512,128]{2,0,1:T(8,128)(2,1)} copy(bf16[16,512,128]{2,1,0:T(8,128)(2,1)} %param.5) | data formatting | bytes 4194304 | tf_op args[0]
  4.3 10.0 %all-to-all-start.1 = ((bf16[16,512,128]{2,0,1:T(8,128)(2,1)}), bf16[16,512,128]{2,0,1:T(8,128)(2,1)S(1)}, u32[]{:S(2)}, u32[]{:S(2)}) async-start(bf16[16,512,128]{2,0,1:T(8,128)(2,1)} %copy.14), calls=%async_computation.1 | async-start | bytes 4194304 | tf_op jit(solution)/shard_map/all_to_all | solution.py:25
  14.3 0.0 copy-done
  14.3 0.1 fusion.34
  14.4 0.2 select_reduce_fusion
  14.6 0.0 copy-done.1
  14.6 0.2 convolution_convert_fusion.1
  14.9 0.1 copy.13
  15.0 0.1 reshape.85
  15.1 0.1 reshape.82
  15.2 0.0 copy-done.2
  15.2 0.0 copy-done.3
  15.2 0.7 fusion.26
  16.0 47.3 %all-to-all-done.1 = bf16[16,512,128]{2,0,1:T(8,128)(2,1)S(1)} async-done(((bf16[16,512,128]{2,0,1:T(8,128)(2,1)}), bf16[16,512,128]{2,0,1:T(8,128)(2,1)S(1)}, u32[]{:S(2)}, u32[]{:S(2)}) %all-to-all-start.1) | async-done | bytes 2097184 | tf_op jit(solution)/shard_map/all_to_all | solution.py:25
  63.3 6.8 %all-to-all-start = ((f32[16,2,3]{2,1,0:T(2,128)}), f32[16,2,3]{2,1,0:T(2,128)S(1)}, u32[]{:S(2)}, u32[]{:S(2)}) async-start(f32[16,2,3]{2,1,0:T(2,128)} %bitcast.2), calls=%async_computation | async-start | bytes 32768 | tf_op jit(solution)/shard_map/all_to_all | solution.py:42
  70.0 1.4 copy.15
  71.4 18.9 %fusion.19 = bf16[2048,512]{0,1:T(8,128)(2,1)S(1)} fusion(bf16[64,8,16,128]{3,2,1,0:T(8,128)(2,1)S(1)} %bitcast.33), kind=kOutput, calls=%fused_computation.27 | convolution fusion | flops 4392484864 | bytes 4194304 | tf_op jit(solution)/shard_map/dot_general | solution.py:27
  90.3 5.4 %gather_fusion = bf16[64,32,2048]{2,1,0:T(8,128)(2,1)} fusion(bf16[16,32,2048]{2,1,0:T(8,128)(2,1)S(1)} %bitcast.29, s32[1024]{0:T(1024)S(1)} %pad_clamp_fusion), kind=kCustom, calls=%fused_computation | custom fusion | bytes 16777472 | tf_op jit(solution)/shard_map/jit(_take)/gather | solution.py:55
  95.7 7.5 %broadcast_select_fusion = bf16[16,4,32,2048]{3,2,1,0:T(8,128)(2,1)} fusion(bf16[16,4,32,2048]{3,2,1,0:T(8,128)(2,1)} %bitcast.30, pred[16,4]{1,0:T(8,128)(4,1)S(1)} %compare_and_fusion), kind=kLoop, calls=%fused_computation.26 | loop fusion | flops 4194304 | bytes 16777280 | tf_op jit(solution)/shard_map/jit(_take)/select_n | solution.py:55
  103.2 0.0 all-to-all-done
  103.2 6.7 %all-to-all-start.2 = ((bf16[16,4,32,2048]{3,2,1,0:T(8,128)(2,1)}), bf16[16,4,32,2048]{3,2,1,0:T(8,128)(2,1)}, u32[]{:S(2)}, u32[]{:S(2)}) async-start(bf16[16,4,32,2048]{3,2,1,0:T(8,128)(2,1)} %broadcast_select_fusion), calls=%async_computation.2 | async-start | bytes 16777216 | tf_op jit(solution)/shard_map/all_to_all | solution.py:58
  109.9 0.3 fusion.25
  110.3 0.1 sub.24
  110.4 0.1 slice.19
  110.4 142.5 %all-to-all-done.2 = bf16[16,4,32,2048]{3,2,1,0:T(8,128)(2,1)} async-done(((bf16[16,4,32,2048]{3,2,1,0:T(8,128)(2,1)}), bf16[16,4,32,2048]{3,2,1,0:T(8,128)(2,1)}, u32[]{:S(2)}, u32[]{:S(2)}) %all-to-all-start.2) | async-done | bytes 8388640 | tf_op jit(solution)/shard_map/all_to_all | solution.py:58
  253.0 21.6 %reshape.86 = bf16[32,2,65536]{2,1,0:T(2,128)(2,1)} reshape(bf16[16,4,32,2048]{3,2,1,0:T(8,128)(2,1)} %all-to-all-done.2) | data formatting | bytes 16777216 | tf_op jit(solution)/shard_map/reshape | solution.py:60
  274.6 10.9 %fusion.27 = bf16[32,1,65536]{2,1,0:T(2,128)(2,1)S(1)} fusion(bf16[32,2,65536]{2,1,0:T(2,128)(2,1)} %reshape.86, bf16[32,2,1]{1,0,2:T(8,128)(2,1)S(1)} %bitcast.34), kind=kOutput, calls=%fused_computation.38 | convolution fusion | flops 8388608 | bytes 12583040 | tf_op jit(solution)/shard_map/sb,sbk->sk/dot_general | solution.py:61
  285.5 4.6 %convolution_convert_fusion = bf16[16,65536]{1,0:T(8,128)(2,1)S(1)} fusion(bf16[32,1,65536]{2,1,0:T(2,128)(2,1)S(1)} %fusion.27, s32[32]{0:T(128)S(1)} %sub.24), kind=kOutput, calls=%fused_computation.1 | convolution fusion | flops 68157952 | bytes 6291584 | tf_op jit(solution)/shard_map/dot_general | solution.py:64
  290.1 2.5 copy.24
  (7 shorter events, 0.1 us)
Async XLA Ops:
  0.0 14.3 %copy-start = (s32[16,1]{0,1:T(1,128)S(1)}, s32[16,1]{0,1:T(1,128)}, u32[]{:S(2)}) copy-start(s32[16,1]{0,1:T(1,128)} %param.6) | copy-start | bytes 196
  0.0 14.6 %copy-start.1 = (s32[16]{0:T(128)S(1)}, s32[16]{0:T(128)}, u32[]{:S(2)}) copy-start(s32[16]{0:T(128)} %param.8) | copy-start | bytes 196
  0.0 15.2 %copy-start.2 = (bf16[16,2]{0,1:T(2,128)(2,1)S(1)}, bf16[16,2]{0,1:T(2,128)(2,1)}, u32[]{:S(2)}) copy-start(bf16[16,2]{0,1:T(2,128)(2,1)} %param.9) | copy-start | bytes 196
  0.0 15.2 %copy-start.3 = (s32[16]{0:T(128)S(1)}, s32[16]{0:T(128)}, u32[]{:S(2)}) copy-start(s32[16]{0:T(128)} %param.7) | copy-start | bytes 196
  4.3 58.9 %all-to-all-start.1 = ((bf16[16,512,128]{2,0,1:T(8,128)(2,1)}), bf16[16,512,128]{2,0,1:T(8,128)(2,1)S(1)}, u32[]{:S(2)}, u32[]{:S(2)}) async-start(bf16[16,512,128]{2,0,1:T(8,128)(2,1)} %copy.14), calls=%async_computation.1 | async-start | bytes 4194304 | tf_op jit(solution)/shard_map/all_to_all | solution.py:25
  63.3 39.9 %all-to-all-start = ((f32[16,2,3]{2,1,0:T(2,128)}), f32[16,2,3]{2,1,0:T(2,128)S(1)}, u32[]{:S(2)}, u32[]{:S(2)}) async-start(f32[16,2,3]{2,1,0:T(2,128)} %bitcast.2), calls=%async_computation | async-start | bytes 32768 | tf_op jit(solution)/shard_map/all_to_all | solution.py:42
  103.2 149.8 %all-to-all-start.2 = ((bf16[16,4,32,2048]{3,2,1,0:T(8,128)(2,1)}), bf16[16,4,32,2048]{3,2,1,0:T(8,128)(2,1)}, u32[]{:S(2)}, u32[]{:S(2)}) async-start(bf16[16,4,32,2048]{3,2,1,0:T(8,128)(2,1)} %broadcast_select_fusion), calls=%async_computation.2 | async-start | bytes 16777216 | tf_op jit(solution)/shard_map/all_to_all | solution.py:58
where the time goes:
time: 297 us; the launch traced here: 293 us
  waiting for transfers between devices  190 us (64%)
  local copies, waits for them, and re-layouts  35.6 us (12%)
  matrix products  35.4 us (12%)
  starting transfers between devices  23.5 us (8%)
  other arithmetic  8.13 us (3%)
    all_to_all x1, waiting for transfers between devices, on_device(): lax.all_to_all(chosen, 'views', split_axis=0, concat_axis=0, tiled=True)  143 us
    all_to_all x1, waiting for transfers between devices, on_device(): lax.all_to_all(grad_par, 'rows', split_axis=1, concat_axis=2, tiled=True)  47.3 us
    reshape x1, local copies, waits for them, and re-layouts, on_device(): paired = received.reshape(slots_all, band_len, rows_here * channels)  21.6 us
    dot_general x1, matrix products, on_device(): jnp.dot(flattened, filter_table, preferred_element_type=jnp.float32)  18.9 us
    dot_general x1, matrix products, on_device(): jnp.einsum('sb,sbk->sk', weights, paired, preferred_element_type=jnp.floa...  10.9 us
    all_to_all x1, starting transfers between devices, on_device(): lax.all_to_all(grad_par, 'rows', split_axis=1, concat_axis=2, tiled=True)  9.98 us
    select_n x2, other arithmetic, on_device(): chosen = jnp.take(filtered, slot_views.reshape(-1), axis=0)  7.46 us
    unnamed x10, local copies, waits for them, and re-layouts  6.8 us
  transfers between devices with their start and end apart: 3, of which 2 were waited for; matrix products, arithmetic and copies ran while one was open for 12% of the time, Pallas kernels for 0%

commit v1 on v0

v1 whole, which is shorter than its diff:
```python
import functools
import math

import jax
import jax.numpy as jnp
import ml_dtypes
import numpy as np
from jax import lax
from jax.experimental import pallas as pl
from jax.experimental.pallas import tpu as pltpu
from jax.sharding import PartitionSpec as P

MESH = pl.DeviceIdType.MESH
BF = jnp.bfloat16
F32 = jnp.float32
I32 = jnp.int32

C = 2048
NV = 16
NR = 16
ROWS = 32
R = 4
N = ROWS // R
FOLD = 16 // R
L = C // FOLD
XY = 4
NZ = 8
LAG = 2

VIEW_OFFS = [(1, 0), (0, 1), (3, 0), (0, 3), (1, 1), (3, 3), (1, 3), (3, 1), (2, 0), (0, 2), (2, 1), (1, 2), (2, 3), (3, 2), (2, 2)]
ROW_OFFS = [(z, c) for z in (1, 7, 2, 6, 3, 5, 4) for c in (0, 1)] + [(0, 1)]


def toeplitz_column():
    m = np.arange(2 * C - 256)[:, None] - np.arange(256)[None, :] - (C - 256)
    distance = np.abs(m)
    far = np.maximum(distance.astype(np.float32), np.float32(1.0))
    odd = np.float32(-4.0) / (np.float32(math.pi**2) * far * far)
    values = np.where(distance == 0, np.float32(1.0), np.where(distance % 2 == 1, odd, np.float32(0.0)))
    return values.astype(ml_dtypes.bfloat16)


def iota(shape, dim):
    return lax.broadcasted_iota(I32, shape, dim)


def wait_for(ref, sem):
    pltpu.make_async_copy(ref, ref, sem).wait()


def kernel(owner_ref, fan_ref, start_ref, wt_ref, x_hbm, g_hbm, out_ref,
           x_in, g, zsrc, zrecv, csrc, fin, raw, msrc, mrecv, wmat, cmat, pmat,
           in_sem, z_send, z_recv, c_send, c_recv, m_send, m_recv):
    v = lax.axis_index("views")
    r = lax.axis_index("rows")
    x, y = v // XY, v % XY
    z, core = r // 2, r % 2

    load_x = pltpu.make_async_copy(x_hbm, x_in, in_sem.at[0])
    load_x.start()
    load_g = pltpu.make_async_copy(g_hbm, g, in_sem.at[1])
    load_g.start()

    def row_peer(dz, dc):
        return ((z + dz) % NZ) * 2 + (core + dc) % 2

    def view_peer(dx, dy):
        return ((x + dx) % XY) * XY + (y + dy) % XY

    barrier = pltpu.get_barrier_semaphore()
    for off in ROW_OFFS:
        pl.semaphore_signal(barrier, inc=1, device_id=(v, row_peer(*off)), device_id_type=MESH)
    for off in VIEW_OFFS:
        pl.semaphore_signal(barrier, inc=1, device_id=(view_peer(*off), r), device_id_type=MESH)

    row, col = iota((256, 256), 0), iota((256, 256), 1)
    pmat[...] = ((row // 16 == col % 16) & (row % 16 == col // 16)).astype(F32).astype(BF)

    load_x.wait()

    def permute(part):
        def pair(i, carry):
            a, b = 2 * i, 2 * i + 1
            blocks = [
                x_in[:, pl.ds(pl.multiple_of(t * ROWS + part * 16, 16), 16), :].reshape(256, 128) for t in (a, b)
            ]
            moved = jnp.dot(pmat[...], jnp.concatenate(blocks, axis=1), preferred_element_type=F32).astype(BF)
            for t, piece in ((a, moved[:, :128]), (b, moved[:, 128:])):
                zsrc[part * FOLD:(part + 1) * FOLD, t] = piece.reshape(FOLD, R * NV, 128)
            return carry

        lax.fori_loop(0, NR // 2, pair, 0)

    def send_rows(c):
        for off in ROW_OFFS:
            t = row_peer(*off)
            pltpu.make_async_remote_copy(
                src_ref=zsrc.at[c, t], dst_ref=zrecv.at[c, r], send_sem=z_send.at[c], recv_sem=z_recv.at[c],
                device_id=(v, t), device_id_type=MESH,
            ).start()
        pltpu.make_async_copy(zsrc.at[c, r], zrecv.at[c, r], z_recv.at[c]).start()

    permute(0)
    pl.semaphore_wait(barrier, len(ROW_OFFS) + len(VIEW_OFFS))
    for c in range(N // 2):
        send_rows(c)
    permute(1)
    for c in range(N // 2, N):
        send_rows(c)

    owners = [owner_ref[k] for k in range(NV)]
    ranks = []
    for k in range(NV):
        rank = jnp.int32(0)
        for j in range(k):
            rank = rank + jnp.where(owners[j] == owners[k], 1, 0).astype(I32)
        ranks.append(rank)
    slots = [owners[k] * 2 + ranks[k] for k in range(NV)]

    shape = (NV, 8, 128)
    slot_of = iota(shape, 0) * 2 + jnp.minimum(iota(shape, 1), 1)
    told = jnp.zeros(shape, F32)
    for k in range(NV):
        told = jnp.where(slot_of == slots[k], (fan_ref[k] + 1).astype(F32), told)
    msrc[...] = told
    for off in VIEW_OFFS:
        o = view_peer(*off)
        pltpu.make_async_remote_copy(
            src_ref=msrc.at[o], dst_ref=mrecv.at[v], send_sem=m_send, recv_sem=m_recv,
            device_id=(o, r), device_id_type=MESH,
        ).start()
    pltpu.make_async_copy(msrc.at[v], mrecv.at[v], m_recv).start()

    shape = (512, 256)
    row_slot = iota(shape, 0) // 16
    view_col = iota((8, 256), 1) % 16
    weights = jnp.zeros(shape, F32)
    for k in range(NV):
        band = jnp.where(
            view_col == start_ref[k], wt_ref[k, 0], jnp.where(view_col == start_ref[k] + 1, wt_ref[k, 1], 0.0)
        )
        weights = jnp.where(row_slot == slots[k], band[0:1, :], weights)
    same = iota(shape, 0) % 16 == iota(shape, 1) // 16
    wmat[...] = jnp.where(same, weights, 0.0).astype(BF)

    wait_for(mrecv, m_recv)
    lane_slot = iota((1, 128), 1) // 16
    for part in range(4):
        target = jnp.zeros((1, 128), F32)
        for s in range(4):
            for slot in range(2):
                target = jnp.where(lane_slot == 2 * s + slot, mrecv[4 * part + s, slot:slot + 1, :], target)
        shape = (256, 128)
        hit = (iota(shape, 0) // 16 + 1).astype(F32) == target
        same = iota(shape, 0) % 16 == iota(shape, 1) % 16
        cmat[:, 128 * part:128 * (part + 1)] = jnp.where(hit & same, 1.0, 0.0).astype(BF)

    load_g.wait()

    def collect(c):
        wait_for(fin.at[c], c_recv.at[c])
        raw[c] = jnp.dot(cmat[...], fin[c].reshape(512, L), preferred_element_type=F32)

    def step(c, carry):
        wait_for(zrecv.at[c], z_recv.at[c])
        lines = jnp.concatenate([zrecv[c, t] for t in range(NR)], axis=1)
        filtered = [
            jnp.dot(lines, g[C - 256 - 256 * j:2 * C - 256 - 256 * j, :], preferred_element_type=F32).astype(BF)
            for j in range(C // 256)
        ]
        per = L // 256
        folded = jnp.concatenate(
            [jnp.concatenate(filtered[q * per:(q + 1) * per], axis=1) for q in range(FOLD)], axis=0
        )
        contrib = jnp.dot(wmat[...], folded, preferred_element_type=F32).astype(BF)
        csrc[c] = contrib.reshape(NV, 32, L)
        for off in VIEW_OFFS:
            o = view_peer(*off)
            pltpu.make_async_remote_copy(
                src_ref=csrc.at[c, o], dst_ref=fin.at[c, v], send_sem=c_send.at[c], recv_sem=c_recv.at[c],
                device_id=(o, r), device_id_type=MESH,
            ).start()
        pltpu.make_async_copy(csrc.at[c, v], fin.at[c, v], c_recv.at[c]).start()

        @pl.when(c >= LAG)
        def _():
            collect(c - LAG)

        return carry

    lax.fori_loop(0, N, step, 0)
    for c in range(N - LAG, N):
        collect(c)

    for group in range(2):
        for q in range(FOLD):
            pieces = [
                raw[c].reshape(NV, 16, L)[:, R * q:R * (q + 1), :] for c in range(group * FOLD, (group + 1) * FOLD)
            ]
            whole = jnp.concatenate(pieces, axis=1)
            out_ref[:, 16 * group:16 * (group + 1), L * q:L * (q + 1)] = whole.astype(BF)

    wait_for(msrc.at[pl.ds(0, NV - 1)], m_send)

    def drain(c, carry):
        wait_for(zsrc.at[c, pl.ds(0, NR - 1)], z_send.at[c])
        wait_for(csrc.at[c, pl.ds(0, NV - 1)], c_send.at[c])
        return carry

    lax.fori_loop(0, N, drain, 0)


def on_device(grad_par, contrib_owner, contrib_fan, contrib_start, contrib_wt):
    smem = pl.BlockSpec(memory_space=pltpu.SMEM)
    anywhere = pl.BlockSpec(memory_space=pl.ANY)
    column = jnp.asarray(toeplitz_column())
    return pl.pallas_call(
        kernel,
        out_shape=jax.ShapeDtypeStruct((NV, ROWS, C), BF),
        in_specs=[smem, smem, smem, smem, anywhere, anywhere],
        out_specs=pl.BlockSpec(memory_space=pltpu.VMEM),
        scratch_shapes=[
            pltpu.VMEM((NV, 512, 128), BF),
            pltpu.VMEM((2 * C - 256, 256), BF),
            pltpu.VMEM((N, NR, R * NV, 128), BF),
            pltpu.VMEM((N, NR, R * NV, 128), BF),
            pltpu.VMEM((N, NV, 32, L), BF),
            pltpu.VMEM((N, NV, 32, L), BF),
            pltpu.VMEM((N, 256, L), F32),
            pltpu.VMEM((NV, 8, 128), F32),
            pltpu.VMEM((NV, 8, 128), F32),
            pltpu.VMEM((512, 256), BF),
            pltpu.VMEM((256, 512), BF),
            pltpu.VMEM((256, 256), BF),
            pltpu.SemaphoreType.DMA((2,)),
            pltpu.SemaphoreType.DMA((N,)),
            pltpu.SemaphoreType.DMA((N,)),
            pltpu.SemaphoreType.DMA((N,)),
            pltpu.SemaphoreType.DMA((N,)),
            pltpu.SemaphoreType.DMA,
            pltpu.SemaphoreType.DMA,
        ],
        compiler_params=pltpu.CompilerParams(
            collective_id=0, has_side_effects=True, vmem_limit_bytes=52 << 20
        ),
    )(contrib_owner[:, 0], contrib_fan, contrib_start, contrib_wt.astype(F32), grad_par, column)


def solution(mesh):
    return jax.shard_map(
        on_device,
        mesh=mesh,
        in_specs=(
            P("views", None, "rows"),
            P("views", None),
            P("views"),
            P("views"),
            P("views", None),
        ),
        out_specs=P("views", "rows", None),
        check_vma=False,
    )
```

time: 297 us -> 82.2 us (0.28); the launches traced: 293 us -> 82 us
  waiting for transfers between devices: 190 us -> 0 us
  Pallas kernels: 0 us -> 74.6 us
  matrix products: 35.4 us -> 0 us
  local copies, waits for them, and re-layouts: 35.6 us -> 7.41 us
  starting transfers between devices: 23.5 us -> 0 us
  other arithmetic: 8.13 us -> 0 us
    all_to_all x3 -> x0, waiting for transfers between devices: 190 us -> none  [the longest x1 143 us: on_device(): lax.all_to_all(chosen, 'views', split_axis=0, concat_axis=0, tiled=True)]
    pallas_call x0 -> x1, Pallas kernels: none -> 74.6 us  [on_device(): pl.pallas_call(kernel, out_shape=jax.ShapeDtypeStruct((NV, ROWS, C), BF),...]
    dot_general x4 -> x0, matrix products: 34.7 us -> none  [the longest x1 18.9 us: on_device(): jnp.dot(flattened, filter_table, preferred_element_type=jnp.float32)]
    all_to_all x3 -> x0, starting transfers between devices: 23.5 us -> none  [the longest x1 9.98 us: on_device(): lax.all_to_all(grad_par, 'rows', split_axis=1, concat_axis=2, tiled=True)]
    reshape x3 -> x0, local copies, waits for them, and re-layouts: 21.8 us -> none  [the longest x1 21.6 us: on_device(): paired = received.reshape(slots_all, band_len, rows_here * channels)]
    select_n x2 -> x0, other arithmetic: 7.46 us -> none  [on_device(): chosen = jnp.take(filtered, slot_views.reshape(-1), axis=0)]
    gather x1 -> x0, local copies, waits for them, and re-layouts: 5.41 us -> none  [on_device(): chosen = jnp.take(filtered, slot_views.reshape(-1), axis=0)]
    unnamed x10 -> x9, local copies, waits for them, and re-layouts: 6.8 us -> 6.67 us
  transfers between devices with their start and end apart: 3 -> 0, of which waited for: 2 -> 0; matrix products, arithmetic and copies ran while one was open for 12% -> 0% of each run, Pallas kernels for 0% -> 0%
where the time goes in v1:
time: 82.2 us; the launch traced here: 82 us
  Pallas kernels  74.6 us (91%)
  local copies, waits for them, and re-layouts  7.41 us (9%)
    pallas_call x1, Pallas kernels, on_device(): pl.pallas_call(kernel, out_shape=jax.ShapeDtypeStruct((NV, ROWS, C), BF),...  74.6 us
    unnamed x9, local copies, waits for them, and re-layouts  6.67 us

profile of v1, /device:TPU:1, one launch (start us, length us, event | category | flops | bytes accessed | tf_op | source)
XLA Modules:
  0.0 82.0 jit_solution(15315748758733814482)
XLA Ops:
  0.0 0.7 copy.8.wt_ref
  0.7 0.0 copy-start
  0.7 1.5 %copy-done = bf16[3840,256]{1,0:T(8,128)(2,1)S(1)} copy-done((bf16[3840,256]{1,0:T(8,128)(2,1)S(1)}, bf16[3840,256]{1,0:T(8,128)(2,1)}, u32[]{:S(2)}) %copy-start) | copy-done | bytes 1966104
  2.3 0.0 copy-start.1
  2.3 0.7 copy-done.1
  2.9 0.0 copy-start.2
  2.9 0.7 copy-done.2
  3.6 0.0 copy-start.3
  3.6 0.7 copy-done.3
  4.3 74.6 %shard_map.64 = bf16[16,32,2048]{2,1,0:T(8,128)(2,1)} custom-call(s32[16]{0:T(128)S(1)} %bitcast.1, s32[16]{0:T(128)S(1)} %copy-done.2, s32[16]{0:T(128)S(1)} %copy-done.3, f32[16,2]{1,0:T(8,128)S(1)} %copy.8.wt_ref, bf16[16,512,128]{2,1,0:T(8,128)(2,1)} %x_hbm.1, bf16[3840,256]{1,0:T(8,128)(2,1)S(1)} %copy-done), custom_call_target="tpu_custom_call" | custom-call | tf_op jit(solution)/shard_map/pallas_call | solution.py:217
  78.8 3.2 %copy.10 = bf16[16,32,2048]{2,1,0:T(8,128)(2,1)} copy(bf16[16,32,2048]{2,1,0:T(8,128)(2,1)} %shard_map.64) | data formatting | bytes 4194304
Async XLA Ops:
  0.7 1.5 %copy-start = (bf16[3840,256]{1,0:T(8,128)(2,1)S(1)}, bf16[3840,256]{1,0:T(8,128)(2,1)}, u32[]{:S(2)}) copy-start(bf16[3840,256]{1,0:T(8,128)(2,1)} %constant.2.clone.g_hbm) | copy-start | bytes 5898244
  2.3 0.7 copy-start.1
  2.9 0.7 copy-start.2
  3.6 0.7 copy-start.3

commit v2 on v1

--- a/solution.py
+++ b/solution.py
@@ -48,18 +48,29 @@
     pltpu.make_async_copy(ref, ref, sem).wait()
 
 
-def kernel(owner_ref, fan_ref, start_ref, wt_ref, x_hbm, g_hbm, out_ref,
-           x_in, g, zsrc, zrecv, csrc, fin, raw, msrc, mrecv, wmat, cmat, pmat,
+def kernel(owner_hbm, fan_hbm, start_hbm, wt_hbm, x_hbm, g_hbm, out_ref,
+           owner_ref, fan_ref, start_ref, wt_ref, x_in, g, zsrc, zrecv, csrc, fin, raw, msrc, mrecv, wmat, cmat, pmat,
            in_sem, z_send, z_recv, c_send, c_recv, m_send, m_recv):
     v = lax.axis_index("views")
     r = lax.axis_index("rows")
     x, y = v // XY, v % XY
     z, core = r // 2, r % 2
 
-    load_x = pltpu.make_async_copy(x_hbm, x_in, in_sem.at[0])
-    load_x.start()
-    load_g = pltpu.make_async_copy(g_hbm, g, in_sem.at[1])
-    load_g.start()
+    load_x = [
+        pltpu.make_async_copy(
+            x_hbm.at[:, 4 * ROWS * i:4 * ROWS * (i + 1), :], x_in.at[:, 4 * ROWS * i:4 * ROWS * (i + 1), :], in_sem.at[i]
+        )
+        for i in range(4)
+    ]
+    load_small = [
+        pltpu.make_async_copy(src, dst, in_sem.at[5 + i])
+        for i, (src, dst) in enumerate(
+            ((owner_hbm, owner_ref), (fan_hbm, fan_ref), (start_hbm, start_ref), (wt_hbm, wt_ref))
+        )
+    ]
+    load_g = pltpu.make_async_copy(g_hbm, g, in_sem.at[4])
+    for copy in load_x + load_small + [load_g]:
+        copy.start()
 
     def row_peer(dz, dc):
         return ((z + dz) % NZ) * 2 + (core + dc) % 2
@@ -76,20 +87,15 @@
     row, col = iota((256, 256), 0), iota((256, 256), 1)
     pmat[...] = ((row // 16 == col % 16) & (row % 16 == col // 16)).astype(F32).astype(BF)
 
-    load_x.wait()
-
     def permute(part):
-        def pair(i, carry):
-            a, b = 2 * i, 2 * i + 1
-            blocks = [
-                x_in[:, pl.ds(pl.multiple_of(t * ROWS + part * 16, 16), 16), :].reshape(256, 128) for t in (a, b)
-            ]
+        for i in range(NR // 2):
+            if part == 0 and i % 2 == 0:
+                load_x[i // 2].wait()
+            pair = (2 * i, 2 * i + 1)
+            blocks = [x_in[:, t * ROWS + part * 16:t * ROWS + part * 16 + 16, :].reshape(256, 128) for t in pair]
             moved = jnp.dot(pmat[...], jnp.concatenate(blocks, axis=1), preferred_element_type=F32).astype(BF)
-            for t, piece in ((a, moved[:, :128]), (b, moved[:, 128:])):
+            for t, piece in zip(pair, (moved[:, :128], moved[:, 128:])):
                 zsrc[part * FOLD:(part + 1) * FOLD, t] = piece.reshape(FOLD, R * NV, 128)
-            return carry
-
-        lax.fori_loop(0, NR // 2, pair, 0)
 
     def send_rows(c):
         for off in ROW_OFFS:
@@ -108,6 +114,8 @@
     for c in range(N // 2, N):
         send_rows(c)
 
+    for copy in load_small:
+        copy.wait()
     owners = [owner_ref[k] for k in range(NV)]
     ranks = []
     for k in range(NV):
@@ -134,10 +142,12 @@
     shape = (512, 256)
     row_slot = iota(shape, 0) // 16
     view_col = iota((8, 256), 1) % 16
+    wt = wt_ref[...].astype(F32)
     weights = jnp.zeros(shape, F32)
     for k in range(NV):
         band = jnp.where(
-            view_col == start_ref[k], wt_ref[k, 0], jnp.where(view_col == start_ref[k] + 1, wt_ref[k, 1], 0.0)
+            view_col == start_ref[k], wt[0:1, k:k + 1],
+            jnp.where(view_col == start_ref[k] + 1, wt[1:2, k:k + 1], 0.0),
         )
         weights = jnp.where(row_slot == slots[k], band[0:1, :], weights)
     same = iota(shape, 0) % 16 == iota(shape, 1) // 16
@@ -189,10 +199,7 @@
         return carry
 
     lax.fori_loop(0, N, step, 0)
-    for c in range(N - LAG, N):
-        collect(c)
-
-    for group in range(2):
+    def unfold(group):
         for q in range(FOLD):
             pieces = [
                 raw[c].reshape(NV, 16, L)[:, R * q:R * (q + 1), :] for c in range(group * FOLD, (group + 1) * FOLD)
@@ -200,6 +207,11 @@
             whole = jnp.concatenate(pieces, axis=1)
             out_ref[:, 16 * group:16 * (group + 1), L * q:L * (q + 1)] = whole.astype(BF)
 
+    unfold(0)
+    for c in range(N - LAG, N):
+        collect(c)
+    unfold(1)
+
     wait_for(msrc.at[pl.ds(0, NV - 1)], m_send)
 
     def drain(c, carry):
@@ -211,15 +223,19 @@
 
 
 def on_device(grad_par, contrib_owner, contrib_fan, contrib_start, contrib_wt):
-    smem = pl.BlockSpec(memory_space=pltpu.SMEM)
-    anywhere = pl.BlockSpec(memory_space=pl.ANY)
+    hbm = pl.BlockSpec(memory_space=pltpu.HBM)
+    vmem = pl.BlockSpec(memory_space=pltpu.VMEM)
     column = jnp.asarray(toeplitz_column())
-    return pl.pallas_call(
+    result = pl.pallas_call(
         kernel,
-        out_shape=jax.ShapeDtypeStruct((NV, ROWS, C), BF),
-        in_specs=[smem, smem, smem, smem, anywhere, anywhere],
-        out_specs=pl.BlockSpec(memory_space=pltpu.VMEM),
+        out_shape=pltpu.VMEM((NV, ROWS, C), BF),
+        in_specs=[hbm] * 6,
+        out_specs=vmem,
         scratch_shapes=[
+            pltpu.SMEM((NV,), I32),
+            pltpu.SMEM((NV,), I32),
+            pltpu.SMEM((NV,), I32),
+            pltpu.VMEM((2, NV), BF),
             pltpu.VMEM((NV, 512, 128), BF),
             pltpu.VMEM((2 * C - 256, 256), BF),
             pltpu.VMEM((N, NR, R * NV, 128), BF),
@@ -232,7 +248,7 @@
             pltpu.VMEM((512, 256), BF),
             pltpu.VMEM((256, 512), BF),
             pltpu.VMEM((256, 256), BF),
-            pltpu.SemaphoreType.DMA((2,)),
+            pltpu.SemaphoreType.DMA((9,)),
             pltpu.SemaphoreType.DMA((N,)),
             pltpu.SemaphoreType.DMA((N,)),
             pltpu.SemaphoreType.DMA((N,)),
@@ -241,9 +257,10 @@
             pltpu.SemaphoreType.DMA,
         ],
         compiler_params=pltpu.CompilerParams(
-            collective_id=0, has_side_effects=True, vmem_limit_bytes=52 << 20
+            collective_id=0, has_side_effects=True, vmem_limit_bytes=61 << 20
         ),
-    )(contrib_owner[:, 0], contrib_fan, contrib_start, contrib_wt.astype(F32), grad_par, column)
+    )(contrib_owner[:, 0], contrib_fan, contrib_start, contrib_wt.T, grad_par, column)
+    return result
 
 
 def solution(mesh):

time: 82.2 us -> 72.8 us (0.89)
  local copies, waits for them, and re-layouts: 7.41 us -> 1.32 us
  Pallas kernels: 74.6 us -> 71.4 us
    unnamed x9 -> x1, local copies, waits for them, and re-layouts: 6.67 us -> 1.32 us
    pallas_call x1, Pallas kernels: 74.6 us -> 71.4 us  [on_device(): pl.pallas_call(kernel, out_shape=pltpu.VMEM((NV, ROWS, C), BF), in_specs=...]
where the time goes in v2:
time: 72.8 us; the launch traced here: 72.7 us
  Pallas kernels  71.4 us (98%)
  local copies, waits for them, and re-layouts  1.32 us (2%)
    pallas_call x1, Pallas kernels, on_device(): pl.pallas_call(kernel, out_shape=pltpu.VMEM((NV, ROWS, C), BF), in_specs=...  71.4 us

profile of v2, /device:TPU:1, one launch (start us, length us, event | category | flops | bytes accessed | tf_op | source)
XLA Modules:
  0.0 72.7 jit_solution(13735760786205231655)
XLA Ops:
  0.0 71.4 %shard_map.64 = bf16[16,32,2048]{2,1,0:T(8,128)(2,1)S(1)} custom-call(s32[16]{0:T(128)} %bitcast.2, s32[16]{0:T(128)} %fan_hbm.1, s32[16]{0:T(128)} %start_hbm.1, bf16[2,16]{1,0:T(2,128)(2,1)} %bitcast.3, bf16[16,512,128]{2,1,0:T(8,128)(2,1)} %x_hbm.1, bf16[3840,256]{1,0:T(8,128)(2,1)} %constant.2.clone.g_hbm), custom_call_target="tpu_custom_call" | custom-call | tf_op jit(solution)/shard_map/pallas_call | solution.py:229
  71.4 1.3 %copy.8 = bf16[16,32,2048]{2,1,0:T(8,128)(2,1)} copy(bf16[16,32,2048]{2,1,0:T(8,128)(2,1)S(1)} %shard_map.64) | data formatting | bytes 4194304

commit v3 on v2

--- a/solution.py
+++ b/solution.py
@@ -19,13 +19,14 @@
 NV = 16
 NR = 16
 ROWS = 32
-R = 4
+R = 2
 N = ROWS // R
 FOLD = 16 // R
 L = C // FOLD
 XY = 4
 NZ = 8
-LAG = 2
+LAG = 4
+AHEAD = 6
 
 VIEW_OFFS = [(1, 0), (0, 1), (3, 0), (0, 3), (1, 1), (3, 3), (1, 3), (3, 1), (2, 0), (0, 2), (2, 1), (1, 2), (2, 3), (3, 2), (2, 2)]
 ROW_OFFS = [(z, c) for z in (1, 7, 2, 6, 3, 5, 4) for c in (0, 1)] + [(0, 1)]
@@ -78,11 +79,14 @@
     def view_peer(dx, dy):
         return ((x + dx) % XY) * XY + (y + dy) % XY
 
+    row_peers = [row_peer(*off) for off in ROW_OFFS]
+    view_peers = [view_peer(*off) for off in VIEW_OFFS]
+
     barrier = pltpu.get_barrier_semaphore()
-    for off in ROW_OFFS:
-        pl.semaphore_signal(barrier, inc=1, device_id=(v, row_peer(*off)), device_id_type=MESH)
-    for off in VIEW_OFFS:
-        pl.semaphore_signal(barrier, inc=1, device_id=(view_peer(*off), r), device_id_type=MESH)
+    for t in row_peers:
+        pl.semaphore_signal(barrier, inc=1, device_id=(v, t), device_id_type=MESH)
+    for o in view_peers:
+        pl.semaphore_signal(barrier, inc=1, device_id=(o, r), device_id_type=MESH)
 
     row, col = iota((256, 256), 0), iota((256, 256), 1)
     pmat[...] = ((row // 16 == col % 16) & (row % 16 == col // 16)).astype(F32).astype(BF)
@@ -98,8 +102,7 @@
                 zsrc[part * FOLD:(part + 1) * FOLD, t] = piece.reshape(FOLD, R * NV, 128)
 
     def send_rows(c):
-        for off in ROW_OFFS:
-            t = row_peer(*off)
+        for t in row_peers:
             pltpu.make_async_remote_copy(
                 src_ref=zsrc.at[c, t], dst_ref=zrecv.at[c, r], send_sem=z_send.at[c], recv_sem=z_recv.at[c],
                 device_id=(v, t), device_id_type=MESH,
@@ -108,10 +111,7 @@
 
     permute(0)
     pl.semaphore_wait(barrier, len(ROW_OFFS) + len(VIEW_OFFS))
-    for c in range(N // 2):
-        send_rows(c)
-    permute(1)
-    for c in range(N // 2, N):
+    for c in range(AHEAD):
         send_rows(c)
 
     for copy in load_small:
@@ -131,8 +131,7 @@
     for k in range(NV):
         told = jnp.where(slot_of == slots[k], (fan_ref[k] + 1).astype(F32), told)
     msrc[...] = told
-    for off in VIEW_OFFS:
-        o = view_peer(*off)
+    for o in view_peers:
         pltpu.make_async_remote_copy(
             src_ref=msrc.at[o], dst_ref=mrecv.at[v], send_sem=m_send, recv_sem=m_recv,
             device_id=(o, r), device_id_type=MESH,
@@ -153,25 +152,26 @@
     same = iota(shape, 0) % 16 == iota(shape, 1) // 16
     wmat[...] = jnp.where(same, weights, 0.0).astype(BF)
 
-    wait_for(mrecv, m_recv)
-    lane_slot = iota((1, 128), 1) // 16
-    for part in range(4):
-        target = jnp.zeros((1, 128), F32)
-        for s in range(4):
-            for slot in range(2):
-                target = jnp.where(lane_slot == 2 * s + slot, mrecv[4 * part + s, slot:slot + 1, :], target)
-        shape = (256, 128)
-        hit = (iota(shape, 0) // 16 + 1).astype(F32) == target
-        same = iota(shape, 0) % 16 == iota(shape, 1) % 16
-        cmat[:, 128 * part:128 * (part + 1)] = jnp.where(hit & same, 1.0, 0.0).astype(BF)
-
     load_g.wait()
 
     def collect(c):
         wait_for(fin.at[c], c_recv.at[c])
         raw[c] = jnp.dot(cmat[...], fin[c].reshape(512, L), preferred_element_type=F32)
 
-    def step(c, carry):
+    def build_sum():
+        wait_for(mrecv, m_recv)
+        lane_slot = iota((1, 128), 1) // 16
+        for part in range(4):
+            target = jnp.zeros((1, 128), F32)
+            for s in range(4):
+                for slot in range(2):
+                    target = jnp.where(lane_slot == 2 * s + slot, mrecv[4 * part + s, slot:slot + 1, :], target)
+            shape = (256, 128)
+            hit = (iota(shape, 0) // 16 + 1).astype(F32) == target
+            same = iota(shape, 0) % 16 == iota(shape, 1) % 16
+            cmat[:, 128 * part:128 * (part + 1)] = jnp.where(hit & same, 1.0, 0.0).astype(BF)
+
+    def step(c, ahead, behind):
         wait_for(zrecv.at[c], z_recv.at[c])
         lines = jnp.concatenate([zrecv[c, t] for t in range(NR)], axis=1)
         filtered = [
@@ -184,21 +184,32 @@
         )
         contrib = jnp.dot(wmat[...], folded, preferred_element_type=F32).astype(BF)
         csrc[c] = contrib.reshape(NV, 32, L)
-        for off in VIEW_OFFS:
-            o = view_peer(*off)
+        for o in view_peers:
             pltpu.make_async_remote_copy(
                 src_ref=csrc.at[c, o], dst_ref=fin.at[c, v], send_sem=c_send.at[c], recv_sem=c_recv.at[c],
                 device_id=(o, r), device_id_type=MESH,
             ).start()
         pltpu.make_async_copy(csrc.at[c, v], fin.at[c, v], c_recv.at[c]).start()
-
-        @pl.when(c >= LAG)
-        def _():
+        if ahead:
+            send_rows(c + AHEAD)
+        if behind:
             collect(c - LAG)
 
-        return carry
-
-    lax.fori_loop(0, N, step, 0)
+    def steps(first, last, ahead, behind):
+        def body(c, carry):
+            step(c, ahead, behind)
+            return carry
+
+        lax.fori_loop(first, last, body, 0)
+
+    turns = sorted({0, N // 2 - AHEAD, LAG, N - AHEAD, N})
+    for first, last in zip(turns, turns[1:]):
+        if first == N // 2 - AHEAD:
+            permute(1)
+        if first == LAG:
+            build_sum()
+        steps(first, last, first < N - AHEAD, first >= LAG)
+
     def unfold(group):
         for q in range(FOLD):
             pieces = [

time: 72.8 us -> 70.9 us (0.974)
  Pallas kernels: 71.4 us -> 69.5 us
    pallas_call x1, Pallas kernels: 71.4 us -> 69.5 us  [on_device(): pl.pallas_call(kernel, out_shape=pltpu.VMEM((NV, ROWS, C), BF), in_specs=...]
where the time goes in v3:
time: 70.9 us; the launch traced here: 70.8 us
  Pallas kernels  69.5 us (98%)
  local copies, waits for them, and re-layouts  1.32 us (2%)
    pallas_call x1, Pallas kernels, on_device(): pl.pallas_call(kernel, out_shape=pltpu.VMEM((NV, ROWS, C), BF), in_specs=...  69.5 us

profile of v3, /device:TPU:1, one launch (start us, length us, event | category | flops | bytes accessed | tf_op | source)
XLA Modules:
  0.0 70.8 jit_solution(3189799114232319569)
XLA Ops:
  0.0 69.5 %shard_map.64 = bf16[16,32,2048]{2,1,0:T(8,128)(2,1)S(1)} custom-call(s32[16]{0:T(128)} %bitcast.2, s32[16]{0:T(128)} %fan_hbm.1, s32[16]{0:T(128)} %start_hbm.1, bf16[2,16]{1,0:T(2,128)(2,1)} %bitcast.3, bf16[16,512,128]{2,1,0:T(8,128)(2,1)} %x_hbm.1, bf16[3840,256]{1,0:T(8,128)(2,1)} %constant.2.clone.g_hbm), custom_call_target="tpu_custom_call" | custom-call | tf_op jit(solution)/shard_map/pallas_call | solution.py:240
  69.5 1.3 %copy.8 = bf16[16,32,2048]{2,1,0:T(8,128)(2,1)} copy(bf16[16,32,2048]{2,1,0:T(8,128)(2,1)S(1)} %shard_map.64) | data formatting | bytes 4194304

commit v4 on v3

--- a/solution.py
+++ b/solution.py
@@ -50,7 +50,7 @@
 
 
 def kernel(owner_hbm, fan_hbm, start_hbm, wt_hbm, x_hbm, g_hbm, out_ref,
-           owner_ref, fan_ref, start_ref, wt_ref, x_in, g, zsrc, zrecv, csrc, fin, raw, msrc, mrecv, wmat, cmat, pmat,
+           owner_ref, fan_ref, start_ref, wt_ref, x_in, g, zsrc, zrecv, csrc, fin, raw, held, msrc, mrecv, wmat, cmat, pmat,
            in_sem, z_send, z_recv, c_send, c_recv, m_send, m_recv):
     v = lax.axis_index("views")
     r = lax.axis_index("rows")
@@ -210,18 +210,16 @@
             build_sum()
         steps(first, last, first < N - AHEAD, first >= LAG)
 
-    def unfold(group):
-        for q in range(FOLD):
-            pieces = [
-                raw[c].reshape(NV, 16, L)[:, R * q:R * (q + 1), :] for c in range(group * FOLD, (group + 1) * FOLD)
-            ]
-            whole = jnp.concatenate(pieces, axis=1)
-            out_ref[:, 16 * group:16 * (group + 1), L * q:L * (q + 1)] = whole.astype(BF)
-
-    unfold(0)
-    for c in range(N - LAG, N):
-        collect(c)
-    unfold(1)
+    def eight_rows(part, q):
+        chunks = range(part * FOLD // 2, (part + 1) * FOLD // 2)
+        return jnp.concatenate([raw[c].reshape(NV, 16, L)[:, R * q:R * (q + 1), :] for c in chunks], axis=1)
+
+    blocks = [slice(L * q, L * (q + 1)) for q in range(FOLD)]
+    for q in range(FOLD):
+        whole = jnp.concatenate([eight_rows(0, q), eight_rows(1, q)], axis=1)
+        out_ref[:, 0:16, blocks[q]] = whole.astype(BF)
+    for q in range(FOLD):
+        held[:, :, blocks[q]] = eight_rows(2, q)
 
     wait_for(msrc.at[pl.ds(0, NV - 1)], m_send)
 
@@ -230,7 +228,13 @@
         wait_for(csrc.at[c, pl.ds(0, NV - 1)], c_send.at[c])
         return carry
 
-    lax.fori_loop(0, N, drain, 0)
+    lax.fori_loop(0, N - LAG, drain, 0)
+    for c in range(N - LAG, N):
+        collect(c)
+    for q in range(FOLD):
+        whole = jnp.concatenate([held[:, :, blocks[q]], eight_rows(3, q)], axis=1)
+        out_ref[:, 16:32, blocks[q]] = whole.astype(BF)
+    lax.fori_loop(N - LAG, N, drain, 0)
 
 
 def on_device(grad_par, contrib_owner, contrib_fan, contrib_start, contrib_wt):
@@ -254,6 +258,7 @@
             pltpu.VMEM((N, NV, 32, L), BF),
             pltpu.VMEM((N, NV, 32, L), BF),
             pltpu.VMEM((N, 256, L), F32),
+            pltpu.VMEM((NV, 8, C), F32),
             pltpu.VMEM((NV, 8, 128), F32),
             pltpu.VMEM((NV, 8, 128), F32),
             pltpu.VMEM((512, 256), BF),

time: 70.9 us -> 70.6 us (level)
  no operation moved by 1% of the time
where the time goes in v4:
time: 70.6 us; the launch traced here: 70.5 us
  Pallas kernels  69.2 us (98%)
  local copies, waits for them, and re-layouts  1.32 us (2%)
    pallas_call x1, Pallas kernels, on_device(): pl.pallas_call(kernel, out_shape=pltpu.VMEM((NV, ROWS, C), BF), in_specs=...  69.2 us

profile of v4, /device:TPU:1, one launch (start us, length us, event | category | flops | bytes accessed | tf_op | source)
XLA Modules:
  0.0 70.5 jit_solution(13412114234158678514)
XLA Ops:
  0.0 69.2 %shard_map.64 = bf16[16,32,2048]{2,1,0:T(8,128)(2,1)S(1)} custom-call(s32[16]{0:T(128)} %bitcast.2, s32[16]{0:T(128)} %fan_hbm.1, s32[16]{0:T(128)} %start_hbm.1, bf16[2,16]{1,0:T(2,128)(2,1)} %bitcast.3, bf16[16,512,128]{2,1,0:T(8,128)(2,1)} %x_hbm.1, bf16[3840,256]{1,0:T(8,128)(2,1)} %constant.2.clone.g_hbm), custom_call_target="tpu_custom_call" | custom-call | tf_op jit(solution)/shard_map/pallas_call | solution.py:244
  69.2 1.3 %copy.8 = bf16[16,32,2048]{2,1,0:T(8,128)(2,1)} copy(bf16[16,32,2048]{2,1,0:T(8,128)(2,1)S(1)} %shard_map.64) | data formatting | bytes 4194304
